TPU v7x, 512 devices: a whole 4x4x16 slice. The times are simulated.
512 devices in a mesh: level: 8 (over x, core), row: 16 (over z), col: 4 (over y).
Axes of the slice: x: 4, y: 4, z: 16, core: 2. Of those that a mesh axis runs over, the one named last changes fastest.
Arguments:
- factor_tiles: bfloat16 [8, 64, 16, 4, 128, 128], P('level', 'row', None, 'col'), may hold values from -0.0625 to 0.0625
- tile_mask: int32 [8, 64, 16, 4], P('level', 'row', None, 'col'), may hold values from 0 to 1, as said below
- inverse_diagonal: bfloat16 [8, 16, 4, 128, 128], P('level', 'row', 'col'), may hold values from -1.5 to 1.5, as said below
- right_sides: float32 [8, 16, 4, 128, 128], P('level', 'row', 'col'), may hold values from -6 to 6
Outputs:
- forward_solution: bfloat16 [8, 16, 4, 128, 128], P('level', 'row', 'col')
- solution: bfloat16 [8, 16, 4, 128, 128], P('level', 'row', 'col')
Inputs may be any that keep to these rules, and one draw needn't show every extreme that they name: `tile_mask`: 1 where the factor holds the tile, 0 where it does not; tiles are present only where |i - j| <= 32 with j = q * 4 + c, a band that follows the elimination tree. `inverse_diagonal`: each 128 x 128 block is lower triangular, the inverse of a diagonal block of the factor.
All inputs are finite; a program needn't handle non-finite values.
Results may differ from a plain program's by a relative error of at most 0.035.
Values may be sent and summed in bfloat16 or wider, within the bound.
A program may use at most 64 MiB of HBM per device.

v0:
```python
import jax
import jax.numpy as jnp
from jax import lax
from jax.sharding import PartitionSpec as P


def shifted(block, axis, distance):
    devices = range(lax.axis_size(axis))
    route = [(i - distance, i) for i in devices if i - distance in devices]
    return lax.ppermute(block, axis, route)


def solve_block(inverse, values):
    return jnp.einsum(
        "kst,ktr->ksr", inverse, values.astype(jnp.bfloat16), preferred_element_type=jnp.float32
    ).astype(jnp.bfloat16)


def solve_transposed(inverse, values):
    return jnp.einsum(
        "kts,ktr->ksr", inverse, values.astype(jnp.bfloat16), preferred_element_type=jnp.float32
    ).astype(jnp.bfloat16)


def local(factor_tiles, tile_mask, inverse_diagonal, right_sides):
    nlev = lax.axis_size("level")
    ncol = lax.axis_size("col")
    masked = factor_tiles[0, :, :, 0] * tile_mask[0, :, :, 0][:, :, None, None].astype(jnp.bfloat16)
    block_rows = masked.shape[0]
    qcount = masked.shape[1]
    side = masked.shape[2]
    own_rows = block_rows // ncol
    masked_split = masked.reshape(own_rows, ncol, qcount, side, side)
    inverse = inverse_diagonal[0, :, 0]
    sides = right_sides[0, :, 0]
    total_cols = sides.shape[-1]
    width, count, split = (total_cols, nlev - 1, 0)
    solved = solve_block(inverse, sides)
    for step in range(1, count + 1):
        piece = solved
        arrived = shifted(piece, "level", 1)
        partial_value = jnp.einsum(
            "aqst,qtr->asr",
            masked,
            lax.all_gather(arrived, "row", axis=0, tiled=True),
            preferred_element_type=jnp.float32,
        )
        pieces = lax.all_to_all(
            partial_value.reshape(own_rows, ncol, side, width).astype(jnp.bfloat16),
            "col",
            split_axis=1,
            concat_axis=1,
            tiled=True,
        ).astype(jnp.float32)
        mine = jnp.sum(pieces, axis=1)
        source = sides
        solved = solve_block(inverse, source - mine)
    answer = solve_transposed(inverse, solved)
    for step in range(1, count + 1):
        piece = answer[:, None]
        fold_piece = lax.all_gather(piece, "col", axis=1, tiled=True)
        partial_value = jnp.einsum(
            "kcqst,kcsr->qtr", masked_split, fold_piece, preferred_element_type=jnp.float32
        )
        summed = lax.psum_scatter(
            partial_value.astype(jnp.bfloat16), "row", scatter_dimension=0, tiled=True
        ).astype(jnp.float32)
        arrived = shifted(summed.astype(jnp.bfloat16), "level", -1).astype(summed.dtype)
        source = solved.astype(jnp.float32)
        answer = solve_transposed(inverse, source - arrived)
    return (solved[None, :, None], answer[None, :, None])


def solution(mesh):
    placed = (
        P("level", "row", None, "col", None, None),
        P("level", "row", None, "col"),
        P("level", "row", "col", None, None),
        P("level", "row", "col", None, None),
    )
    return jax.shard_map(
        local,
        mesh=mesh,
        in_specs=placed,
        out_specs=(P("level", "row", "col", None, None), P("level", "row", "col", None, None)),
        check_vma=False,
    )
```

profile of v0, /device:TPU:1, one launch (start us, length us, event | category | flops | bytes accessed | tf_op | source)
XLA Modules:
  0.0 923.1 jit_solution(2617397229417016310)
XLA Ops:
  17.8 28.6 %all_gather.42 = bf16[16,128,128]{2,1,0:T(8,128)(2,1)S(1)} all-gather(bf16[1,128,128]{2,1,0:T(8,128)(2,1)S(1)} %collective-permute-done), channel_id=1, replica_groups=mesh['level'=8,'row'=16,'col'=4] {'row'}, dimensions={0}, use_global_device_ids=true | all-gather | bytes 557056 | tf_op jit(solution)/shard_map/all_gather | solution.py:45
  57.9 12.0 %collective-permute-start.1 = (bf16[1,128,128]{1,2,0:T(8,128)(2,1)S(1)}, bf16[1,128,128]{1,2,0:T(8,128)(2,1)S(1)}, u32[]{:S(2)}, u32[]{:S(2)}) collective-permute-start(bf16[1,128,128]{1,2,0:T(8,128)(2,1)S(1)} %fusion.71), channel_id=1, source_target_pairs={{0,64},{64,128},{128,192},{192,256},{256,320},{320,384},{384,448},... | collective-permute-start | bytes 98312 | tf_op jit(solution)/shard_map/ppermute | solution.py:10
  71.0 22.7 %all_gather.43 = bf16[16,128,128]{2,1,0:T(8,128)(2,1)S(1)} all-gather(bf16[1,128,128]{2,1,0:T(8,128)(2,1)S(1)} %copy.36), channel_id=1, replica_groups=mesh['level'=8,'row'=16,'col'=4] {'row'}, dimensions={0}, use_global_device_ids=true | all-gather | bytes 557056 | tf_op jit(solution)/shard_map/all_gather | solution.py:45
  101.9 12.0 %collective-permute-start.2 = (bf16[1,128,128]{1,2,0:T(8,128)(2,1)S(1)}, bf16[1,128,128]{1,2,0:T(8,128)(2,1)S(1)}, u32[]{:S(2)}, u32[]{:S(2)}) collective-permute-start(bf16[1,128,128]{1,2,0:T(8,128)(2,1)S(1)} %fusion.72), channel_id=1, source_target_pairs={{0,64},{64,128},{128,192},{192,256},{256,320},{320,384},{384,448},... | collective-permute-start | bytes 98312 | tf_op jit(solution)/shard_map/ppermute | solution.py:10
  115.0 23.8 %all_gather.44 = bf16[16,128,128]{2,1,0:T(8,128)(2,1)S(1)} all-gather(bf16[1,128,128]{2,1,0:T(8,128)(2,1)S(1)} %copy.38), channel_id=1, replica_groups=mesh['level'=8,'row'=16,'col'=4] {'row'}, dimensions={0}, use_global_device_ids=true | all-gather | bytes 557056 | tf_op jit(solution)/shard_map/all_gather | solution.py:45
  147.9 11.6 %collective-permute-start.3 = (bf16[1,128,128]{1,2,0:T(8,128)(2,1)S(1)}, bf16[1,128,128]{1,2,0:T(8,128)(2,1)S(1)}, u32[]{:S(2)}, u32[]{:S(2)}) collective-permute-start(bf16[1,128,128]{1,2,0:T(8,128)(2,1)S(1)} %fusion.73), channel_id=1, source_target_pairs={{0,64},{64,128},{128,192},{192,256},{256,320},{320,384},{384,448},... | collective-permute-start | bytes 98312 | tf_op jit(solution)/shard_map/ppermute | solution.py:10
  160.7 22.7 %all_gather.45 = bf16[16,128,128]{2,1,0:T(8,128)(2,1)S(1)} all-gather(bf16[1,128,128]{2,1,0:T(8,128)(2,1)S(1)} %copy.40), channel_id=1, replica_groups=mesh['level'=8,'row'=16,'col'=4] {'row'}, dimensions={0}, use_global_device_ids=true | all-gather | bytes 557056 | tf_op jit(solution)/shard_map/all_gather | solution.py:45
  191.6 11.7 %collective-permute-start.4 = (bf16[1,128,128]{1,2,0:T(8,128)(2,1)S(1)}, bf16[1,128,128]{1,2,0:T(8,128)(2,1)S(1)}, u32[]{:S(2)}, u32[]{:S(2)}) collective-permute-start(bf16[1,128,128]{1,2,0:T(8,128)(2,1)S(1)} %fusion.74), channel_id=1, source_target_pairs={{0,64},{64,128},{128,192},{192,256},{256,320},{320,384},{384,448},... | collective-permute-start | bytes 98312 | tf_op jit(solution)/shard_map/ppermute | solution.py:10
  204.4 23.7 %all_gather.46 = bf16[16,128,128]{2,1,0:T(8,128)(2,1)S(1)} all-gather(bf16[1,128,128]{2,1,0:T(8,128)(2,1)S(1)} %copy.42), channel_id=1, replica_groups=mesh['level'=8,'row'=16,'col'=4] {'row'}, dimensions={0}, use_global_device_ids=true | all-gather | bytes 557056 | tf_op jit(solution)/shard_map/all_gather | solution.py:45
  236.2 12.5 %collective-permute-start.5 = (bf16[1,128,128]{1,2,0:T(8,128)(2,1)S(1)}, bf16[1,128,128]{1,2,0:T(8,128)(2,1)S(1)}, u32[]{:S(2)}, u32[]{:S(2)}) collective-permute-start(bf16[1,128,128]{1,2,0:T(8,128)(2,1)S(1)} %fusion.75), channel_id=1, source_target_pairs={{0,64},{64,128},{128,192},{192,256},{256,320},{320,384},{384,448},... | collective-permute-start | bytes 98312 | tf_op jit(solution)/shard_map/ppermute | solution.py:10
  249.8 22.7 %all_gather.47 = bf16[16,128,128]{2,1,0:T(8,128)(2,1)S(1)} all-gather(bf16[1,128,128]{2,1,0:T(8,128)(2,1)S(1)} %copy.44), channel_id=1, replica_groups=mesh['level'=8,'row'=16,'col'=4] {'row'}, dimensions={0}, use_global_device_ids=true | all-gather | bytes 557056 | tf_op jit(solution)/shard_map/all_gather | solution.py:45
  280.8 12.4 %collective-permute-start.6 = (bf16[1,128,128]{1,2,0:T(8,128)(2,1)S(1)}, bf16[1,128,128]{1,2,0:T(8,128)(2,1)S(1)}, u32[]{:S(2)}, u32[]{:S(2)}) collective-permute-start(bf16[1,128,128]{1,2,0:T(8,128)(2,1)S(1)} %fusion.76), channel_id=1, source_target_pairs={{0,64},{64,128},{128,192},{192,256},{256,320},{320,384},{384,448},... | collective-permute-start | bytes 98312 | tf_op jit(solution)/shard_map/ppermute | solution.py:10
  294.2 23.5 %all_gather.48 = bf16[16,128,128]{2,1,0:T(8,128)(2,1)S(1)} all-gather(bf16[1,128,128]{2,1,0:T(8,128)(2,1)S(1)} %copy.46), channel_id=1, replica_groups=mesh['level'=8,'row'=16,'col'=4] {'row'}, dimensions={0}, use_global_device_ids=true | all-gather | bytes 557056 | tf_op jit(solution)/shard_map/all_gather | solution.py:45
  336.1 64.7 %reduce-scatter.8.cloned.1.call-done = bf16[1,128,128]{1,2,0:T(8,128)(2,1)} async-done(((bf16[16,128,128]{1,2,0:T(8,128)(2,1)}), bf16[1,128,128]{1,2,0:T(8,128)(2,1)}) %reduce-scatter.8.cloned.1.call-update) | async-done | bytes 32784 | tf_op jit(solution)/shard_map/reduce_scatter | solution.py:65
  400.8 13.2 %collective-permute-start.7 = (bf16[1,128,128]{1,2,0:T(8,128)(2,1)}, bf16[1,128,128]{1,2,0:T(8,128)(2,1)S(1)}, u32[]{:S(2)}, u32[]{:S(2)}) collective-permute-start(bf16[1,128,128]{1,2,0:T(8,128)(2,1)} %reduce-scatter.8.cloned.1.call-done), channel_id=1, source_target_pairs={{64,0},{128,64},{192,128},{256,192},{320,256},{384,320},{448,384},... | collective-permute-start | bytes 98312 | tf_op jit(solution)/shard_map/ppermute | solution.py:10
  427.9 55.9 %reduce-scatter.10.cloned.1.call-done = bf16[1,128,128]{1,2,0:T(8,128)(2,1)} async-done(((bf16[16,128,128]{1,2,0:T(8,128)(2,1)}), bf16[1,128,128]{1,2,0:T(8,128)(2,1)}) %reduce-scatter.10.cloned.1.call-update) | async-done | bytes 32784 | tf_op jit(solution)/shard_map/reduce_scatter | solution.py:65
  483.8 13.3 %collective-permute-start.8 = (bf16[1,128,128]{1,2,0:T(8,128)(2,1)}, bf16[1,128,128]{1,2,0:T(8,128)(2,1)S(1)}, u32[]{:S(2)}, u32[]{:S(2)}) collective-permute-start(bf16[1,128,128]{1,2,0:T(8,128)(2,1)} %reduce-scatter.10.cloned.1.call-done), channel_id=1, source_target_pairs={{64,0},{128,64},{192,128},{256,192},{320,256},{384,320},{448,384},... | collective-permute-start | bytes 98312 | tf_op jit(solution)/shard_map/ppermute | solution.py:10
  500.0 9.4 %all-gather.2 = bf16[512,128]{0,1:T(8,128)(2,1)S(1)} all-gather(bf16[128,128]{0,1:T(8,128)(2,1)S(1)} %fusion.79), channel_id=4, replica_groups=mesh['level'=8,'row'=16,'col'=4] {'col'}, dimensions={0}, use_global_device_ids=true | all-gather | bytes 163840 | tf_op jit(solution)/shard_map/all_gather | solution.py:61
  511.0 55.9 %reduce-scatter.12.cloned.1.call-done = bf16[1,128,128]{1,2,0:T(8,128)(2,1)} async-done(((bf16[16,128,128]{1,2,0:T(8,128)(2,1)}), bf16[1,128,128]{1,2,0:T(8,128)(2,1)}) %reduce-scatter.12.cloned.1.call-update) | async-done | bytes 32784 | tf_op jit(solution)/shard_map/reduce_scatter | solution.py:65
  566.9 13.2 %collective-permute-start.9 = (bf16[1,128,128]{1,2,0:T(8,128)(2,1)}, bf16[1,128,128]{1,2,0:T(8,128)(2,1)S(1)}, u32[]{:S(2)}, u32[]{:S(2)}) collective-permute-start(bf16[1,128,128]{1,2,0:T(8,128)(2,1)} %reduce-scatter.12.cloned.1.call-done), channel_id=1, source_target_pairs={{64,0},{128,64},{192,128},{256,192},{320,256},{384,320},{448,384},... | collective-permute-start | bytes 98312 | tf_op jit(solution)/shard_map/ppermute | solution.py:10
  583.1 9.4 %all-gather.3 = bf16[512,128]{0,1:T(8,128)(2,1)S(1)} all-gather(bf16[128,128]{0,1:T(8,128)(2,1)S(1)} %fusion.80), channel_id=5, replica_groups=mesh['level'=8,'row'=16,'col'=4] {'col'}, dimensions={0}, use_global_device_ids=true | all-gather | bytes 163840 | tf_op jit(solution)/shard_map/all_gather | solution.py:61
  594.1 55.3 %reduce-scatter.14.cloned.1.call-done = bf16[1,128,128]{1,2,0:T(8,128)(2,1)} async-done(((bf16[16,128,128]{1,2,0:T(8,128)(2,1)}), bf16[1,128,128]{1,2,0:T(8,128)(2,1)}) %reduce-scatter.14.cloned.1.call-update) | async-done | bytes 32784 | tf_op jit(solution)/shard_map/reduce_scatter | solution.py:65
  649.4 13.9 %collective-permute-start.10 = (bf16[1,128,128]{1,2,0:T(8,128)(2,1)}, bf16[1,128,128]{1,2,0:T(8,128)(2,1)S(1)}, u32[]{:S(2)}, u32[]{:S(2)}) collective-permute-start(bf16[1,128,128]{1,2,0:T(8,128)(2,1)} %reduce-scatter.14.cloned.1.call-done), channel_id=1, source_target_pairs={{64,0},{128,64},{192,128},{256,192},{320,256},{384,320},{448,384},... | collective-permute-start | bytes 98312 | tf_op jit(solution)/shard_map/ppermute | solution.py:10
  666.2 9.5 %all-gather.4 = bf16[512,128]{0,1:T(8,128)(2,1)S(1)} all-gather(bf16[128,128]{0,1:T(8,128)(2,1)S(1)} %fusion.81), channel_id=6, replica_groups=mesh['level'=8,'row'=16,'col'=4] {'col'}, dimensions={0}, use_global_device_ids=true | all-gather | bytes 163840 | tf_op jit(solution)/shard_map/all_gather | solution.py:61
  677.2 55.5 %reduce-scatter.16.cloned.1.call-done = bf16[1,128,128]{1,2,0:T(8,128)(2,1)} async-done(((bf16[16,128,128]{1,2,0:T(8,128)(2,1)}), bf16[1,128,128]{1,2,0:T(8,128)(2,1)}) %reduce-scatter.16.cloned.1.call-update) | async-done | bytes 32784 | tf_op jit(solution)/shard_map/reduce_scatter | solution.py:65
  732.8 13.6 %collective-permute-start.11 = (bf16[1,128,128]{1,2,0:T(8,128)(2,1)}, bf16[1,128,128]{1,2,0:T(8,128)(2,1)S(1)}, u32[]{:S(2)}, u32[]{:S(2)}) collective-permute-start(bf16[1,128,128]{1,2,0:T(8,128)(2,1)} %reduce-scatter.16.cloned.1.call-done), channel_id=1, source_target_pairs={{64,0},{128,64},{192,128},{256,192},{320,256},{384,320},{448,384},... | collective-permute-start | bytes 98312 | tf_op jit(solution)/shard_map/ppermute | solution.py:10
  749.4 9.5 %all-gather.5 = bf16[512,128]{0,1:T(8,128)(2,1)S(1)} all-gather(bf16[128,128]{0,1:T(8,128)(2,1)S(1)} %fusion.82), channel_id=7, replica_groups=mesh['level'=8,'row'=16,'col'=4] {'col'}, dimensions={0}, use_global_device_ids=true | all-gather | bytes 163840 | tf_op jit(solution)/shard_map/all_gather | solution.py:61
  760.4 55.8 %reduce-scatter.18.cloned.1.call-done = bf16[1,128,128]{1,2,0:T(8,128)(2,1)} async-done(((bf16[16,128,128]{1,2,0:T(8,128)(2,1)}), bf16[1,128,128]{1,2,0:T(8,128)(2,1)}) %reduce-scatter.18.cloned.1.call-update) | async-done | bytes 32784 | tf_op jit(solution)/shard_map/reduce_scatter | solution.py:65
  816.2 13.2 %collective-permute-start.12 = (bf16[1,128,128]{1,2,0:T(8,128)(2,1)}, bf16[1,128,128]{1,2,0:T(8,128)(2,1)S(1)}, u32[]{:S(2)}, u32[]{:S(2)}) collective-permute-start(bf16[1,128,128]{1,2,0:T(8,128)(2,1)} %reduce-scatter.18.cloned.1.call-done), channel_id=1, source_target_pairs={{64,0},{128,64},{192,128},{256,192},{320,256},{384,320},{448,384},... | collective-permute-start | bytes 98312 | tf_op jit(solution)/shard_map/ppermute | solution.py:10
  832.4 9.5 %all-gather.6 = bf16[512,128]{0,1:T(8,128)(2,1)S(1)} all-gather(bf16[128,128]{0,1:T(8,128)(2,1)S(1)} %fusion.83), channel_id=8, replica_groups=mesh['level'=8,'row'=16,'col'=4] {'col'}, dimensions={0}, use_global_device_ids=true | all-gather | bytes 163840 | tf_op jit(solution)/shard_map/all_gather | solution.py:61
  843.4 55.8 %reduce-scatter.20.cloned.1.call-done = bf16[1,128,128]{1,2,0:T(8,128)(2,1)} async-done(((bf16[16,128,128]{1,2,0:T(8,128)(2,1)}), bf16[1,128,128]{1,2,0:T(8,128)(2,1)}) %reduce-scatter.20.cloned.1.call-update) | async-done | bytes 32784 | tf_op jit(solution)/shard_map/reduce_scatter | solution.py:65
  899.2 13.2 %collective-permute-start.13 = (bf16[1,128,128]{1,2,0:T(8,128)(2,1)}, bf16[1,128,128]{1,2,0:T(8,128)(2,1)S(1)}, u32[]{:S(2)}, u32[]{:S(2)}) collective-permute-start(bf16[1,128,128]{1,2,0:T(8,128)(2,1)} %reduce-scatter.20.cloned.1.call-done), channel_id=1, source_target_pairs={{64,0},{128,64},{192,128},{256,192},{320,256},{384,320},{448,384},... | collective-permute-start | bytes 98312 | tf_op jit(solution)/shard_map/ppermute | solution.py:10
  (98 shorter events, 128.9 us)
Async XLA Ops:
  7.2 0.8 copy-start
  7.2 393.6 %reduce-scatter.8.cloned.1.call-start = ((), (), s32[]{:S(2)}) async-start(), calls=%async_computation.14 | async-start | bytes 557056 | tf_op jit(solution)/shard_map/reduce_scatter | solution.py:65
  8.9 8.9 collective-permute-start
  46.3 11.3 %copy-start.1 = (f32[1,1,1,128,128]{4,3,2,1,0:T(8,128)S(1)}, f32[1,1,1,128,128]{4,3,2,1,0:T(8,128)}, u32[]{:S(2)}) copy-start(f32[1,1,1,128,128]{4,3,2,1,0:T(8,128)} %param.7) | copy-start | bytes 196612
  46.3 47.4 %copy-start.2 = (bf16[1,4,16,1,128,128]{5,4,3,2,1,0:T(8,128)(2,1)S(1)}, bf16[1,4,16,1,128,128]{5,4,3,2,1,0:T(8,128)(2,1)}, u32[]{:S(2)}) copy-start(bf16[1,4,16,1,128,128]{5,4,3,2,1,0:T(8,128)(2,1)} %param.4) | copy-start | bytes 6291460
  57.9 13.0 %collective-permute-start.1 = (bf16[1,128,128]{1,2,0:T(8,128)(2,1)S(1)}, bf16[1,128,128]{1,2,0:T(8,128)(2,1)S(1)}, u32[]{:S(2)}, u32[]{:S(2)}) collective-permute-start(bf16[1,128,128]{1,2,0:T(8,128)(2,1)S(1)} %fusion.71), channel_id=1, source_target_pairs={{0,64},{64,128},{128,192},{192,256},{256,320},{320,384},{384,448},... | collective-permute-start | bytes 98312 | tf_op jit(solution)/shard_map/ppermute | solution.py:10
  101.9 13.0 %collective-permute-start.2 = (bf16[1,128,128]{1,2,0:T(8,128)(2,1)S(1)}, bf16[1,128,128]{1,2,0:T(8,128)(2,1)S(1)}, u32[]{:S(2)}, u32[]{:S(2)}) collective-permute-start(bf16[1,128,128]{1,2,0:T(8,128)(2,1)S(1)} %fusion.72), channel_id=1, source_target_pairs={{0,64},{64,128},{128,192},{192,256},{256,320},{320,384},{384,448},... | collective-permute-start | bytes 98312 | tf_op jit(solution)/shard_map/ppermute | solution.py:10
  147.9 12.6 %collective-permute-start.3 = (bf16[1,128,128]{1,2,0:T(8,128)(2,1)S(1)}, bf16[1,128,128]{1,2,0:T(8,128)(2,1)S(1)}, u32[]{:S(2)}, u32[]{:S(2)}) collective-permute-start(bf16[1,128,128]{1,2,0:T(8,128)(2,1)S(1)} %fusion.73), channel_id=1, source_target_pairs={{0,64},{64,128},{128,192},{192,256},{256,320},{320,384},{384,448},... | collective-permute-start | bytes 98312 | tf_op jit(solution)/shard_map/ppermute | solution.py:10
  191.6 12.7 %collective-permute-start.4 = (bf16[1,128,128]{1,2,0:T(8,128)(2,1)S(1)}, bf16[1,128,128]{1,2,0:T(8,128)(2,1)S(1)}, u32[]{:S(2)}, u32[]{:S(2)}) collective-permute-start(bf16[1,128,128]{1,2,0:T(8,128)(2,1)S(1)} %fusion.74), channel_id=1, source_target_pairs={{0,64},{64,128},{128,192},{192,256},{256,320},{320,384},{384,448},... | collective-permute-start | bytes 98312 | tf_op jit(solution)/shard_map/ppermute | solution.py:10
  236.2 13.5 %collective-permute-start.5 = (bf16[1,128,128]{1,2,0:T(8,128)(2,1)S(1)}, bf16[1,128,128]{1,2,0:T(8,128)(2,1)S(1)}, u32[]{:S(2)}, u32[]{:S(2)}) collective-permute-start(bf16[1,128,128]{1,2,0:T(8,128)(2,1)S(1)} %fusion.75), channel_id=1, source_target_pairs={{0,64},{64,128},{128,192},{192,256},{256,320},{320,384},{384,448},... | collective-permute-start | bytes 98312 | tf_op jit(solution)/shard_map/ppermute | solution.py:10
  280.8 13.4 %collective-permute-start.6 = (bf16[1,128,128]{1,2,0:T(8,128)(2,1)S(1)}, bf16[1,128,128]{1,2,0:T(8,128)(2,1)S(1)}, u32[]{:S(2)}, u32[]{:S(2)}) collective-permute-start(bf16[1,128,128]{1,2,0:T(8,128)(2,1)S(1)} %fusion.76), channel_id=1, source_target_pairs={{0,64},{64,128},{128,192},{192,256},{256,320},{320,384},{384,448},... | collective-permute-start | bytes 98312 | tf_op jit(solution)/shard_map/ppermute | solution.py:10
  336.0 147.8 %reduce-scatter.10.cloned.1.call-start = ((), (), s32[]{:S(2)}) async-start(), calls=%async_computation.15 | async-start | bytes 557056 | tf_op jit(solution)/shard_map/reduce_scatter | solution.py:65
  400.8 16.1 %collective-permute-start.7 = (bf16[1,128,128]{1,2,0:T(8,128)(2,1)}, bf16[1,128,128]{1,2,0:T(8,128)(2,1)S(1)}, u32[]{:S(2)}, u32[]{:S(2)}) collective-permute-start(bf16[1,128,128]{1,2,0:T(8,128)(2,1)} %reduce-scatter.8.cloned.1.call-done), channel_id=1, source_target_pairs={{64,0},{128,64},{192,128},{256,192},{320,256},{384,320},{448,384},... | collective-permute-start | bytes 98312 | tf_op jit(solution)/shard_map/ppermute | solution.py:10
  427.9 139.0 %reduce-scatter.12.cloned.1.call-start = ((), (), s32[]{:S(2)}) async-start(), calls=%async_computation.16 | async-start | bytes 557056 | tf_op jit(solution)/shard_map/reduce_scatter | solution.py:65
  483.8 16.1 %collective-permute-start.8 = (bf16[1,128,128]{1,2,0:T(8,128)(2,1)}, bf16[1,128,128]{1,2,0:T(8,128)(2,1)S(1)}, u32[]{:S(2)}, u32[]{:S(2)}) collective-permute-start(bf16[1,128,128]{1,2,0:T(8,128)(2,1)} %reduce-scatter.10.cloned.1.call-done), channel_id=1, source_target_pairs={{64,0},{128,64},{192,128},{256,192},{320,256},{384,320},{448,384},... | collective-permute-start | bytes 98312 | tf_op jit(solution)/shard_map/ppermute | solution.py:10
  510.9 138.5 %reduce-scatter.14.cloned.1.call-start = ((), (), s32[]{:S(2)}) async-start(), calls=%async_computation.17 | async-start | bytes 557056 | tf_op jit(solution)/shard_map/reduce_scatter | solution.py:65
  566.9 16.1 %collective-permute-start.9 = (bf16[1,128,128]{1,2,0:T(8,128)(2,1)}, bf16[1,128,128]{1,2,0:T(8,128)(2,1)S(1)}, u32[]{:S(2)}, u32[]{:S(2)}) collective-permute-start(bf16[1,128,128]{1,2,0:T(8,128)(2,1)} %reduce-scatter.12.cloned.1.call-done), channel_id=1, source_target_pairs={{64,0},{128,64},{192,128},{256,192},{320,256},{384,320},{448,384},... | collective-permute-start | bytes 98312 | tf_op jit(solution)/shard_map/ppermute | solution.py:10
  594.0 138.7 %reduce-scatter.16.cloned.1.call-start = ((), (), s32[]{:S(2)}) async-start(), calls=%async_computation.18 | async-start | bytes 557056 | tf_op jit(solution)/shard_map/reduce_scatter | solution.py:65
  649.4 16.7 %collective-permute-start.10 = (bf16[1,128,128]{1,2,0:T(8,128)(2,1)}, bf16[1,128,128]{1,2,0:T(8,128)(2,1)S(1)}, u32[]{:S(2)}, u32[]{:S(2)}) collective-permute-start(bf16[1,128,128]{1,2,0:T(8,128)(2,1)} %reduce-scatter.14.cloned.1.call-done), channel_id=1, source_target_pairs={{64,0},{128,64},{192,128},{256,192},{320,256},{384,320},{448,384},... | collective-permute-start | bytes 98312 | tf_op jit(solution)/shard_map/ppermute | solution.py:10
  677.2 139.0 %reduce-scatter.18.cloned.1.call-start = ((), (), s32[]{:S(2)}) async-start(), calls=%async_computation.19 | async-start | bytes 557056 | tf_op jit(solution)/shard_map/reduce_scatter | solution.py:65
  732.8 16.5 %collective-permute-start.11 = (bf16[1,128,128]{1,2,0:T(8,128)(2,1)}, bf16[1,128,128]{1,2,0:T(8,128)(2,1)S(1)}, u32[]{:S(2)}, u32[]{:S(2)}) collective-permute-start(bf16[1,128,128]{1,2,0:T(8,128)(2,1)} %reduce-scatter.16.cloned.1.call-done), channel_id=1, source_target_pairs={{64,0},{128,64},{192,128},{256,192},{320,256},{384,320},{448,384},... | collective-permute-start | bytes 98312 | tf_op jit(solution)/shard_map/ppermute | solution.py:10
  760.4 138.8 %reduce-scatter.20.cloned.1.call-start = ((), (), s32[]{:S(2)}) async-start(), calls=%async_computation.20 | async-start | bytes 557056 | tf_op jit(solution)/shard_map/reduce_scatter | solution.py:65
  816.2 16.1 %collective-permute-start.12 = (bf16[1,128,128]{1,2,0:T(8,128)(2,1)}, bf16[1,128,128]{1,2,0:T(8,128)(2,1)S(1)}, u32[]{:S(2)}, u32[]{:S(2)}) collective-permute-start(bf16[1,128,128]{1,2,0:T(8,128)(2,1)} %reduce-scatter.18.cloned.1.call-done), channel_id=1, source_target_pairs={{64,0},{128,64},{192,128},{256,192},{320,256},{384,320},{448,384},... | collective-permute-start | bytes 98312 | tf_op jit(solution)/shard_map/ppermute | solution.py:10
  899.2 16.2 %collective-permute-start.13 = (bf16[1,128,128]{1,2,0:T(8,128)(2,1)}, bf16[1,128,128]{1,2,0:T(8,128)(2,1)S(1)}, u32[]{:S(2)}, u32[]{:S(2)}) collective-permute-start(bf16[1,128,128]{1,2,0:T(8,128)(2,1)} %reduce-scatter.20.cloned.1.call-done), channel_id=1, source_target_pairs={{64,0},{128,64},{192,128},{256,192},{320,256},{384,320},{448,384},... | collective-permute-start | bytes 98312 | tf_op jit(solution)/shard_map/ppermute | solution.py:10
Sparse Core Ops, SparseCore 0:
  336.1 64.5 reduce-scatter.7
  428.0 55.7 reduce-scatter.9
  511.0 55.7 reduce-scatter.11
  594.1 55.2 reduce-scatter.13
  677.3 55.4 reduce-scatter.15
  760.5 55.6 reduce-scatter.17
  843.5 55.6 reduce-scatter.19
where the time goes:
time: 924 us; the launch traced here: 923 us
  waiting for transfers between devices  428 us (46%)
  blocking collectives  286 us (31%)
  starting transfers between devices  170 us (18%)
  matrix products  19.6 us (2%)
  between operations  14.5 us (2%)
    reduce_scatter x7, waiting for transfers between devices, local(): lax.psum_scatter(partial_value.astype(jnp.bfloat16), 'row', scatter_dimen...  399 us
    ppermute x14, starting transfers between devices, shifted(): return lax.ppermute(block, axis, route)  170 us
    all_gather x7, blocking collectives, local(): lax.all_gather(arrived, 'row', axis=0, tiled=True)  168 us
    all_gather x7, blocking collectives, local(): fold_piece = lax.all_gather(piece, 'col', axis=1, tiled=True)  65.2 us
    all_to_all x7, blocking collectives, local(): lax.all_to_all(partial_value.reshape(own_rows, ncol, side, width).astype(...  53 us
    ppermute x14, waiting for transfers between devices, shifted(): return lax.ppermute(block, axis, route)  29.1 us
  transfers between devices with their start and end apart: 21, of which 21 were waited for; matrix products, arithmetic and copies ran while one was open for 0% of the time, Pallas kernels for 0%

commit v1 on v0

--- a/solution.py
+++ b/solution.py
@@ -2,6 +2,13 @@
 import jax.numpy as jnp
 from jax import lax
 from jax.sharding import PartitionSpec as P
+
+
+def exchange_gather(shard, axis, dim):
+    n_dev = lax.axis_size(axis)
+    blocks = jnp.stack([shard for _ in range(n_dev)])
+    blocks = lax.all_to_all(blocks, axis, split_axis=0, concat_axis=0)
+    return jnp.concatenate(blocks, axis=dim)
 
 
 def shifted(block, axis, distance):
@@ -58,7 +65,7 @@
     answer = solve_transposed(inverse, solved)
     for step in range(1, count + 1):
         piece = answer[:, None]
-        fold_piece = lax.all_gather(piece, "col", axis=1, tiled=True)
+        fold_piece = exchange_gather(piece, "col", 1)
         partial_value = jnp.einsum(
             "kcqst,kcsr->qtr", masked_split, fold_piece, preferred_element_type=jnp.float32
         )

time: 924 us -> 910 us (0.985)
  waiting for transfers between devices: 428 us -> 418 us
    all_gather x7 -> x0, blocking collectives: 65.2 us -> none  [local(): fold_piece = lax.all_gather(piece, 'col', axis=1, tiled=True)]
    all_to_all x0 -> x7, blocking collectives: none -> 59.2 us  [exchange_gather(): blocks = lax.all_to_all(blocks, axis, split_axis=0, concat_axis=0)]
    reduce_scatter x7, waiting for transfers between devices: 399 us -> 389 us  [local(): lax.psum_scatter(partial_value.astype(jnp.bfloat16), 'row', scatter_dimen...]
where the time goes in v1:
time: 910 us; the launch traced here: 909 us
  waiting for transfers between devices  418 us (46%)
  blocking collectives  280 us (31%)
  starting transfers between devices  172 us (19%)
  matrix products  19.5 us (2%)
  between operations  14.5 us (2%)
    reduce_scatter x7, waiting for transfers between devices, local(): lax.psum_scatter(partial_value.astype(jnp.bfloat16), 'row', scatter_dimen...  389 us
    ppermute x14, starting transfers between devices, shifted(): return lax.ppermute(block, axis, route)  172 us
    all_gather x7, blocking collectives, local(): lax.all_gather(arrived, 'row', axis=0, tiled=True)  168 us
    all_to_all x7, blocking collectives, exchange_gather(): blocks = lax.all_to_all(blocks, axis, split_axis=0, concat_axis=0)  59.2 us
    all_to_all x7, blocking collectives, local(): lax.all_to_all(partial_value.reshape(own_rows, ncol, side, width).astype(...  53 us
    ppermute x14, waiting for transfers between devices, shifted(): return lax.ppermute(block, axis, route)  28.8 us
  transfers between devices with their start and end apart: 21, of which 21 were waited for; matrix products, arithmetic and copies ran while one was open for 0% of the time, Pallas kernels for 0%

profile of v1, /device:TPU:1, one launch (start us, length us, event | category | flops | bytes accessed | tf_op | source)
XLA Modules:
  0.0 908.5 jit_solution(8010556495176849007)
XLA Ops:
  17.8 28.6 %all_gather.21 = bf16[16,128,128]{2,1,0:T(8,128)(2,1)S(1)} all-gather(bf16[1,128,128]{2,1,0:T(8,128)(2,1)S(1)} %collective-permute-done), channel_id=1, replica_groups=mesh['level'=8,'row'=16,'col'=4] {'row'}, dimensions={0}, use_global_device_ids=true | all-gather | bytes 557056 | tf_op jit(solution)/shard_map/all_gather | solution.py:52
  48.8 8.8 all_to_all.70
  57.9 12.0 %collective-permute-start.1 = (bf16[1,128,128]{1,2,0:T(8,128)(2,1)S(1)}, bf16[1,128,128]{1,2,0:T(8,128)(2,1)S(1)}, u32[]{:S(2)}, u32[]{:S(2)}) collective-permute-start(bf16[1,128,128]{1,2,0:T(8,128)(2,1)S(1)} %fusion.71), channel_id=1, source_target_pairs={{0,64},{64,128},{128,192},{192,256},{256,320},{320,384},{384,448},... | collective-permute-start | bytes 98312 | tf_op jit(solution)/shard_map/ppermute | solution.py:17
  71.0 22.7 %all_gather.22 = bf16[16,128,128]{2,1,0:T(8,128)(2,1)S(1)} all-gather(bf16[1,128,128]{2,1,0:T(8,128)(2,1)S(1)} %copy.36), channel_id=1, replica_groups=mesh['level'=8,'row'=16,'col'=4] {'row'}, dimensions={0}, use_global_device_ids=true | all-gather | bytes 557056 | tf_op jit(solution)/shard_map/all_gather | solution.py:52
  101.9 12.0 %collective-permute-start.2 = (bf16[1,128,128]{1,2,0:T(8,128)(2,1)S(1)}, bf16[1,128,128]{1,2,0:T(8,128)(2,1)S(1)}, u32[]{:S(2)}, u32[]{:S(2)}) collective-permute-start(bf16[1,128,128]{1,2,0:T(8,128)(2,1)S(1)} %fusion.72), channel_id=1, source_target_pairs={{0,64},{64,128},{128,192},{192,256},{256,320},{320,384},{384,448},... | collective-permute-start | bytes 98312 | tf_op jit(solution)/shard_map/ppermute | solution.py:17
  115.0 23.8 %all_gather.23 = bf16[16,128,128]{2,1,0:T(8,128)(2,1)S(1)} all-gather(bf16[1,128,128]{2,1,0:T(8,128)(2,1)S(1)} %copy.38), channel_id=1, replica_groups=mesh['level'=8,'row'=16,'col'=4] {'row'}, dimensions={0}, use_global_device_ids=true | all-gather | bytes 557056 | tf_op jit(solution)/shard_map/all_gather | solution.py:52
  147.9 11.6 %collective-permute-start.3 = (bf16[1,128,128]{1,2,0:T(8,128)(2,1)S(1)}, bf16[1,128,128]{1,2,0:T(8,128)(2,1)S(1)}, u32[]{:S(2)}, u32[]{:S(2)}) collective-permute-start(bf16[1,128,128]{1,2,0:T(8,128)(2,1)S(1)} %fusion.73), channel_id=1, source_target_pairs={{0,64},{64,128},{128,192},{192,256},{256,320},{320,384},{384,448},... | collective-permute-start | bytes 98312 | tf_op jit(solution)/shard_map/ppermute | solution.py:17
  160.7 22.7 %all_gather.24 = bf16[16,128,128]{2,1,0:T(8,128)(2,1)S(1)} all-gather(bf16[1,128,128]{2,1,0:T(8,128)(2,1)S(1)} %copy.40), channel_id=1, replica_groups=mesh['level'=8,'row'=16,'col'=4] {'row'}, dimensions={0}, use_global_device_ids=true | all-gather | bytes 557056 | tf_op jit(solution)/shard_map/all_gather | solution.py:52
  191.6 11.7 %collective-permute-start.4 = (bf16[1,128,128]{1,2,0:T(8,128)(2,1)S(1)}, bf16[1,128,128]{1,2,0:T(8,128)(2,1)S(1)}, u32[]{:S(2)}, u32[]{:S(2)}) collective-permute-start(bf16[1,128,128]{1,2,0:T(8,128)(2,1)S(1)} %fusion.74), channel_id=1, source_target_pairs={{0,64},{64,128},{128,192},{192,256},{256,320},{320,384},{384,448},... | collective-permute-start | bytes 98312 | tf_op jit(solution)/shard_map/ppermute | solution.py:17
  204.4 23.7 %all_gather.25 = bf16[16,128,128]{2,1,0:T(8,128)(2,1)S(1)} all-gather(bf16[1,128,128]{2,1,0:T(8,128)(2,1)S(1)} %copy.42), channel_id=1, replica_groups=mesh['level'=8,'row'=16,'col'=4] {'row'}, dimensions={0}, use_global_device_ids=true | all-gather | bytes 557056 | tf_op jit(solution)/shard_map/all_gather | solution.py:52
  236.2 12.5 %collective-permute-start.5 = (bf16[1,128,128]{1,2,0:T(8,128)(2,1)S(1)}, bf16[1,128,128]{1,2,0:T(8,128)(2,1)S(1)}, u32[]{:S(2)}, u32[]{:S(2)}) collective-permute-start(bf16[1,128,128]{1,2,0:T(8,128)(2,1)S(1)} %fusion.75), channel_id=1, source_target_pairs={{0,64},{64,128},{128,192},{192,256},{256,320},{320,384},{384,448},... | collective-permute-start | bytes 98312 | tf_op jit(solution)/shard_map/ppermute | solution.py:17
  249.8 22.7 %all_gather.26 = bf16[16,128,128]{2,1,0:T(8,128)(2,1)S(1)} all-gather(bf16[1,128,128]{2,1,0:T(8,128)(2,1)S(1)} %copy.44), channel_id=1, replica_groups=mesh['level'=8,'row'=16,'col'=4] {'row'}, dimensions={0}, use_global_device_ids=true | all-gather | bytes 557056 | tf_op jit(solution)/shard_map/all_gather | solution.py:52
  280.8 12.4 %collective-permute-start.6 = (bf16[1,128,128]{1,2,0:T(8,128)(2,1)S(1)}, bf16[1,128,128]{1,2,0:T(8,128)(2,1)S(1)}, u32[]{:S(2)}, u32[]{:S(2)}) collective-permute-start(bf16[1,128,128]{1,2,0:T(8,128)(2,1)S(1)} %fusion.76), channel_id=1, source_target_pairs={{0,64},{64,128},{128,192},{192,256},{256,320},{320,384},{384,448},... | collective-permute-start | bytes 98312 | tf_op jit(solution)/shard_map/ppermute | solution.py:17
  294.2 23.5 %all_gather.27 = bf16[16,128,128]{2,1,0:T(8,128)(2,1)S(1)} all-gather(bf16[1,128,128]{2,1,0:T(8,128)(2,1)S(1)} %copy.46), channel_id=1, replica_groups=mesh['level'=8,'row'=16,'col'=4] {'row'}, dimensions={0}, use_global_device_ids=true | all-gather | bytes 557056 | tf_op jit(solution)/shard_map/all_gather | solution.py:52
  334.8 61.1 %reduce-scatter.8.cloned.1.call-done = bf16[1,128,128]{1,2,0:T(8,128)(2,1)} async-done(((bf16[16,128,128]{1,2,0:T(8,128)(2,1)}), bf16[1,128,128]{1,2,0:T(8,128)(2,1)}) %reduce-scatter.8.cloned.1.call-update) | async-done | bytes 32784 | tf_op jit(solution)/shard_map/reduce_scatter | solution.py:72
  395.9 14.1 %collective-permute-start.7 = (bf16[1,128,128]{1,2,0:T(8,128)(2,1)}, bf16[1,128,128]{1,2,0:T(8,128)(2,1)S(1)}, u32[]{:S(2)}, u32[]{:S(2)}) collective-permute-start(bf16[1,128,128]{1,2,0:T(8,128)(2,1)} %reduce-scatter.8.cloned.1.call-done), channel_id=1, source_target_pairs={{64,0},{128,64},{192,128},{256,192},{320,256},{384,320},{448,384},... | collective-permute-start | bytes 98312 | tf_op jit(solution)/shard_map/ppermute | solution.py:17
  423.2 54.6 %reduce-scatter.10.cloned.1.call-done = bf16[1,128,128]{1,2,0:T(8,128)(2,1)} async-done(((bf16[16,128,128]{1,2,0:T(8,128)(2,1)}), bf16[1,128,128]{1,2,0:T(8,128)(2,1)}) %reduce-scatter.10.cloned.1.call-update) | async-done | bytes 32784 | tf_op jit(solution)/shard_map/reduce_scatter | solution.py:72
  477.8 13.7 %collective-permute-start.8 = (bf16[1,128,128]{1,2,0:T(8,128)(2,1)}, bf16[1,128,128]{1,2,0:T(8,128)(2,1)S(1)}, u32[]{:S(2)}, u32[]{:S(2)}) collective-permute-start(bf16[1,128,128]{1,2,0:T(8,128)(2,1)} %reduce-scatter.10.cloned.1.call-done), channel_id=1, source_target_pairs={{64,0},{128,64},{192,128},{256,192},{320,256},{384,320},{448,384},... | collective-permute-start | bytes 98312 | tf_op jit(solution)/shard_map/ppermute | solution.py:17
  494.6 8.7 all_to_all.79
  504.6 55.2 %reduce-scatter.12.cloned.1.call-done = bf16[1,128,128]{1,2,0:T(8,128)(2,1)} async-done(((bf16[16,128,128]{1,2,0:T(8,128)(2,1)}), bf16[1,128,128]{1,2,0:T(8,128)(2,1)}) %reduce-scatter.12.cloned.1.call-update) | async-done | bytes 32784 | tf_op jit(solution)/shard_map/reduce_scatter | solution.py:72
  559.8 12.9 %collective-permute-start.9 = (bf16[1,128,128]{1,2,0:T(8,128)(2,1)}, bf16[1,128,128]{1,2,0:T(8,128)(2,1)S(1)}, u32[]{:S(2)}, u32[]{:S(2)}) collective-permute-start(bf16[1,128,128]{1,2,0:T(8,128)(2,1)} %reduce-scatter.12.cloned.1.call-done), channel_id=1, source_target_pairs={{64,0},{128,64},{192,128},{256,192},{320,256},{384,320},{448,384},... | collective-permute-start | bytes 98312 | tf_op jit(solution)/shard_map/ppermute | solution.py:17
  585.9 54.2 %reduce-scatter.14.cloned.1.call-done = bf16[1,128,128]{1,2,0:T(8,128)(2,1)} async-done(((bf16[16,128,128]{1,2,0:T(8,128)(2,1)}), bf16[1,128,128]{1,2,0:T(8,128)(2,1)}) %reduce-scatter.14.cloned.1.call-update) | async-done | bytes 32784 | tf_op jit(solution)/shard_map/reduce_scatter | solution.py:72
  640.1 13.9 %collective-permute-start.10 = (bf16[1,128,128]{1,2,0:T(8,128)(2,1)}, bf16[1,128,128]{1,2,0:T(8,128)(2,1)S(1)}, u32[]{:S(2)}, u32[]{:S(2)}) collective-permute-start(bf16[1,128,128]{1,2,0:T(8,128)(2,1)} %reduce-scatter.14.cloned.1.call-done), channel_id=1, source_target_pairs={{64,0},{128,64},{192,128},{256,192},{320,256},{384,320},{448,384},... | collective-permute-start | bytes 98312 | tf_op jit(solution)/shard_map/ppermute | solution.py:17
  657.1 8.7 all_to_all.81
  667.1 54.1 %reduce-scatter.16.cloned.1.call-done = bf16[1,128,128]{1,2,0:T(8,128)(2,1)} async-done(((bf16[16,128,128]{1,2,0:T(8,128)(2,1)}), bf16[1,128,128]{1,2,0:T(8,128)(2,1)}) %reduce-scatter.16.cloned.1.call-update) | async-done | bytes 32784 | tf_op jit(solution)/shard_map/reduce_scatter | solution.py:72
  721.3 13.9 %collective-permute-start.11 = (bf16[1,128,128]{1,2,0:T(8,128)(2,1)}, bf16[1,128,128]{1,2,0:T(8,128)(2,1)S(1)}, u32[]{:S(2)}, u32[]{:S(2)}) collective-permute-start(bf16[1,128,128]{1,2,0:T(8,128)(2,1)} %reduce-scatter.16.cloned.1.call-done), channel_id=1, source_target_pairs={{64,0},{128,64},{192,128},{256,192},{320,256},{384,320},{448,384},... | collective-permute-start | bytes 98312 | tf_op jit(solution)/shard_map/ppermute | solution.py:17
  738.3 8.7 all_to_all.82
  748.4 54.9 %reduce-scatter.18.cloned.1.call-done = bf16[1,128,128]{1,2,0:T(8,128)(2,1)} async-done(((bf16[16,128,128]{1,2,0:T(8,128)(2,1)}), bf16[1,128,128]{1,2,0:T(8,128)(2,1)}) %reduce-scatter.18.cloned.1.call-update) | async-done | bytes 32784 | tf_op jit(solution)/shard_map/reduce_scatter | solution.py:72
  803.3 13.2 %collective-permute-start.12 = (bf16[1,128,128]{1,2,0:T(8,128)(2,1)}, bf16[1,128,128]{1,2,0:T(8,128)(2,1)S(1)}, u32[]{:S(2)}, u32[]{:S(2)}) collective-permute-start(bf16[1,128,128]{1,2,0:T(8,128)(2,1)} %reduce-scatter.18.cloned.1.call-done), channel_id=1, source_target_pairs={{64,0},{128,64},{192,128},{256,192},{320,256},{384,320},{448,384},... | collective-permute-start | bytes 98312 | tf_op jit(solution)/shard_map/ppermute | solution.py:17
  819.7 8.7 all_to_all.83
  829.7 54.6 %reduce-scatter.20.cloned.1.call-done = bf16[1,128,128]{1,2,0:T(8,128)(2,1)} async-done(((bf16[16,128,128]{1,2,0:T(8,128)(2,1)}), bf16[1,128,128]{1,2,0:T(8,128)(2,1)}) %reduce-scatter.20.cloned.1.call-update) | async-done | bytes 32784 | tf_op jit(solution)/shard_map/reduce_scatter | solution.py:72
  884.3 13.6 %collective-permute-start.13 = (bf16[1,128,128]{1,2,0:T(8,128)(2,1)}, bf16[1,128,128]{1,2,0:T(8,128)(2,1)S(1)}, u32[]{:S(2)}, u32[]{:S(2)}) collective-permute-start(bf16[1,128,128]{1,2,0:T(8,128)(2,1)} %reduce-scatter.20.cloned.1.call-done), channel_id=1, source_target_pairs={{64,0},{128,64},{192,128},{256,192},{320,256},{384,320},{448,384},... | collective-permute-start | bytes 98312 | tf_op jit(solution)/shard_map/ppermute | solution.py:17
  (105 shorter events, 126.6 us)
Async XLA Ops:
  7.2 0.8 copy-start
  7.2 388.7 %reduce-scatter.8.cloned.1.call-start = ((), (), s32[]{:S(2)}) async-start(), calls=%async_computation.21 | async-start | bytes 557056 | tf_op jit(solution)/shard_map/reduce_scatter | solution.py:72
  8.9 8.9 collective-permute-start
  46.3 11.3 %copy-start.1 = (f32[1,1,1,128,128]{4,3,2,1,0:T(8,128)S(1)}, f32[1,1,1,128,128]{4,3,2,1,0:T(8,128)}, u32[]{:S(2)}) copy-start(f32[1,1,1,128,128]{4,3,2,1,0:T(8,128)} %param.7) | copy-start | bytes 196612
  46.3 47.4 %copy-start.2 = (bf16[1,4,16,1,128,128]{5,4,3,2,1,0:T(8,128)(2,1)S(1)}, bf16[1,4,16,1,128,128]{5,4,3,2,1,0:T(8,128)(2,1)}, u32[]{:S(2)}) copy-start(bf16[1,4,16,1,128,128]{5,4,3,2,1,0:T(8,128)(2,1)} %param.4) | copy-start | bytes 6291460
  57.9 13.0 %collective-permute-start.1 = (bf16[1,128,128]{1,2,0:T(8,128)(2,1)S(1)}, bf16[1,128,128]{1,2,0:T(8,128)(2,1)S(1)}, u32[]{:S(2)}, u32[]{:S(2)}) collective-permute-start(bf16[1,128,128]{1,2,0:T(8,128)(2,1)S(1)} %fusion.71), channel_id=1, source_target_pairs={{0,64},{64,128},{128,192},{192,256},{256,320},{320,384},{384,448},... | collective-permute-start | bytes 98312 | tf_op jit(solution)/shard_map/ppermute | solution.py:17
  101.9 13.0 %collective-permute-start.2 = (bf16[1,128,128]{1,2,0:T(8,128)(2,1)S(1)}, bf16[1,128,128]{1,2,0:T(8,128)(2,1)S(1)}, u32[]{:S(2)}, u32[]{:S(2)}) collective-permute-start(bf16[1,128,128]{1,2,0:T(8,128)(2,1)S(1)} %fusion.72), channel_id=1, source_target_pairs={{0,64},{64,128},{128,192},{192,256},{256,320},{320,384},{384,448},... | collective-permute-start | bytes 98312 | tf_op jit(solution)/shard_map/ppermute | solution.py:17
  147.9 12.6 %collective-permute-start.3 = (bf16[1,128,128]{1,2,0:T(8,128)(2,1)S(1)}, bf16[1,128,128]{1,2,0:T(8,128)(2,1)S(1)}, u32[]{:S(2)}, u32[]{:S(2)}) collective-permute-start(bf16[1,128,128]{1,2,0:T(8,128)(2,1)S(1)} %fusion.73), channel_id=1, source_target_pairs={{0,64},{64,128},{128,192},{192,256},{256,320},{320,384},{384,448},... | collective-permute-start | bytes 98312 | tf_op jit(solution)/shard_map/ppermute | solution.py:17
  191.6 12.7 %collective-permute-start.4 = (bf16[1,128,128]{1,2,0:T(8,128)(2,1)S(1)}, bf16[1,128,128]{1,2,0:T(8,128)(2,1)S(1)}, u32[]{:S(2)}, u32[]{:S(2)}) collective-permute-start(bf16[1,128,128]{1,2,0:T(8,128)(2,1)S(1)} %fusion.74), channel_id=1, source_target_pairs={{0,64},{64,128},{128,192},{192,256},{256,320},{320,384},{384,448},... | collective-permute-start | bytes 98312 | tf_op jit(solution)/shard_map/ppermute | solution.py:17
  236.2 13.5 %collective-permute-start.5 = (bf16[1,128,128]{1,2,0:T(8,128)(2,1)S(1)}, bf16[1,128,128]{1,2,0:T(8,128)(2,1)S(1)}, u32[]{:S(2)}, u32[]{:S(2)}) collective-permute-start(bf16[1,128,128]{1,2,0:T(8,128)(2,1)S(1)} %fusion.75), channel_id=1, source_target_pairs={{0,64},{64,128},{128,192},{192,256},{256,320},{320,384},{384,448},... | collective-permute-start | bytes 98312 | tf_op jit(solution)/shard_map/ppermute | solution.py:17
  280.8 13.4 %collective-permute-start.6 = (bf16[1,128,128]{1,2,0:T(8,128)(2,1)S(1)}, bf16[1,128,128]{1,2,0:T(8,128)(2,1)S(1)}, u32[]{:S(2)}, u32[]{:S(2)}) collective-permute-start(bf16[1,128,128]{1,2,0:T(8,128)(2,1)S(1)} %fusion.76), channel_id=1, source_target_pairs={{0,64},{64,128},{128,192},{192,256},{256,320},{320,384},{384,448},... | collective-permute-start | bytes 98312 | tf_op jit(solution)/shard_map/ppermute | solution.py:17
  334.8 143.0 %reduce-scatter.10.cloned.1.call-start = ((), (), s32[]{:S(2)}) async-start(), calls=%async_computation.22 | async-start | bytes 557056 | tf_op jit(solution)/shard_map/reduce_scatter | solution.py:72
  395.9 16.9 %collective-permute-start.7 = (bf16[1,128,128]{1,2,0:T(8,128)(2,1)}, bf16[1,128,128]{1,2,0:T(8,128)(2,1)S(1)}, u32[]{:S(2)}, u32[]{:S(2)}) collective-permute-start(bf16[1,128,128]{1,2,0:T(8,128)(2,1)} %reduce-scatter.8.cloned.1.call-done), channel_id=1, source_target_pairs={{64,0},{128,64},{192,128},{256,192},{320,256},{384,320},{448,384},... | collective-permute-start | bytes 98312 | tf_op jit(solution)/shard_map/ppermute | solution.py:17
  423.1 136.7 %reduce-scatter.12.cloned.1.call-start = ((), (), s32[]{:S(2)}) async-start(), calls=%async_computation.23 | async-start | bytes 557056 | tf_op jit(solution)/shard_map/reduce_scatter | solution.py:72
  477.8 16.5 %collective-permute-start.8 = (bf16[1,128,128]{1,2,0:T(8,128)(2,1)}, bf16[1,128,128]{1,2,0:T(8,128)(2,1)S(1)}, u32[]{:S(2)}, u32[]{:S(2)}) collective-permute-start(bf16[1,128,128]{1,2,0:T(8,128)(2,1)} %reduce-scatter.10.cloned.1.call-done), channel_id=1, source_target_pairs={{64,0},{128,64},{192,128},{256,192},{320,256},{384,320},{448,384},... | collective-permute-start | bytes 98312 | tf_op jit(solution)/shard_map/ppermute | solution.py:17
  504.6 135.5 %reduce-scatter.14.cloned.1.call-start = ((), (), s32[]{:S(2)}) async-start(), calls=%async_computation.24 | async-start | bytes 557056 | tf_op jit(solution)/shard_map/reduce_scatter | solution.py:72
  559.8 15.8 %collective-permute-start.9 = (bf16[1,128,128]{1,2,0:T(8,128)(2,1)}, bf16[1,128,128]{1,2,0:T(8,128)(2,1)S(1)}, u32[]{:S(2)}, u32[]{:S(2)}) collective-permute-start(bf16[1,128,128]{1,2,0:T(8,128)(2,1)} %reduce-scatter.12.cloned.1.call-done), channel_id=1, source_target_pairs={{64,0},{128,64},{192,128},{256,192},{320,256},{384,320},{448,384},... | collective-permute-start | bytes 98312 | tf_op jit(solution)/shard_map/ppermute | solution.py:17
  585.9 135.4 %reduce-scatter.16.cloned.1.call-start = ((), (), s32[]{:S(2)}) async-start(), calls=%async_computation.25 | async-start | bytes 557056 | tf_op jit(solution)/shard_map/reduce_scatter | solution.py:72
  640.1 16.7 %collective-permute-start.10 = (bf16[1,128,128]{1,2,0:T(8,128)(2,1)}, bf16[1,128,128]{1,2,0:T(8,128)(2,1)S(1)}, u32[]{:S(2)}, u32[]{:S(2)}) collective-permute-start(bf16[1,128,128]{1,2,0:T(8,128)(2,1)} %reduce-scatter.14.cloned.1.call-done), channel_id=1, source_target_pairs={{64,0},{128,64},{192,128},{256,192},{320,256},{384,320},{448,384},... | collective-permute-start | bytes 98312 | tf_op jit(solution)/shard_map/ppermute | solution.py:17
  667.1 136.2 %reduce-scatter.18.cloned.1.call-start = ((), (), s32[]{:S(2)}) async-start(), calls=%async_computation.26 | async-start | bytes 557056 | tf_op jit(solution)/shard_map/reduce_scatter | solution.py:72
  721.3 16.7 %collective-permute-start.11 = (bf16[1,128,128]{1,2,0:T(8,128)(2,1)}, bf16[1,128,128]{1,2,0:T(8,128)(2,1)S(1)}, u32[]{:S(2)}, u32[]{:S(2)}) collective-permute-start(bf16[1,128,128]{1,2,0:T(8,128)(2,1)} %reduce-scatter.16.cloned.1.call-done), channel_id=1, source_target_pairs={{64,0},{128,64},{192,128},{256,192},{320,256},{384,320},{448,384},... | collective-permute-start | bytes 98312 | tf_op jit(solution)/shard_map/ppermute | solution.py:17
  748.3 136.0 %reduce-scatter.20.cloned.1.call-start = ((), (), s32[]{:S(2)}) async-start(), calls=%async_computation.27 | async-start | bytes 557056 | tf_op jit(solution)/shard_map/reduce_scatter | solution.py:72
  803.3 16.1 %collective-permute-start.12 = (bf16[1,128,128]{1,2,0:T(8,128)(2,1)}, bf16[1,128,128]{1,2,0:T(8,128)(2,1)S(1)}, u32[]{:S(2)}, u32[]{:S(2)}) collective-permute-start(bf16[1,128,128]{1,2,0:T(8,128)(2,1)} %reduce-scatter.18.cloned.1.call-done), channel_id=1, source_target_pairs={{64,0},{128,64},{192,128},{256,192},{320,256},{384,320},{448,384},... | collective-permute-start | bytes 98312 | tf_op jit(solution)/shard_map/ppermute | solution.py:17
  884.3 16.5 %collective-permute-start.13 = (bf16[1,128,128]{1,2,0:T(8,128)(2,1)}, bf16[1,128,128]{1,2,0:T(8,128)(2,1)S(1)}, u32[]{:S(2)}, u32[]{:S(2)}) collective-permute-start(bf16[1,128,128]{1,2,0:T(8,128)(2,1)} %reduce-scatter.20.cloned.1.call-done), channel_id=1, source_target_pairs={{64,0},{128,64},{192,128},{256,192},{320,256},{384,320},{448,384},... | collective-permute-start | bytes 98312 | tf_op jit(solution)/shard_map/ppermute | solution.py:17
Sparse Core Ops, SparseCore 0:
  334.9 60.9 reduce-scatter.7
  423.2 54.4 reduce-scatter.9
  504.7 55.0 reduce-scatter.11
  586.0 54.0 reduce-scatter.13
  667.2 54.0 reduce-scatter.15
  748.4 54.8 reduce-scatter.17
  829.8 54.4 reduce-scatter.19
